TPU v7x, 32 devices: a whole 2x2x4 slice. The times are simulated.
32 devices in a mesh: rows: 16 (over z, y, x), cols: 2 (over core).
Axes of the slice: x: 2, y: 2, z: 4, core: 2. Of those that a mesh axis runs over, the one named last changes fastest.
Arguments:
- panels: float32 [12288, 2, 768], P('rows', None, 'cols'), as said below
- closure_cols: int32 [128, 12], P('rows'), may hold values from -1 to 15, as said below
Outputs:
- factor: float32 [12288, 2, 768], P('rows', None, 'cols')
Inputs may be any that keep to these rules, and one draw needn't show every extreme that they name: `closure_cols`: each entry is a block column 0 to 15 of the two supernodes or -1 for an empty slot; entries may repeat; the supernodes' own rows are not read. The block (rows 0 to 767 of panel 0) and the 1536 by 1536 matrix formed by it and rows 768 to 1535 of both panels, mirrored, is symmetric positive definite.
All inputs are finite; a program needn't handle non-finite values.
Results may differ from a plain program's by a relative error of at most 0.000092.
Values sent between devices are 32-bit elements; how exact they have to be, the bound alone decides.
A program may use at most 128 MiB of HBM per device.

v0:
```python
import jax
import jax.numpy as jnp
from jax import lax
from jax.sharding import PartitionSpec as P

B = 96
S = 8
R = 8


def broadcast(block, axis, holder):
    block = jnp.where(lax.axis_index(axis) == holder, block, jnp.zeros_like(block))
    return lax.psum(block, axis)


def product(left, right):
    return jnp.dot(left, right, precision=lax.Precision.HIGHEST, preferred_element_type=jnp.float32)


def upper_inverse(matrix):
    lower = jnp.linalg.cholesky(matrix)
    identity = jnp.eye(matrix.shape[0], dtype=jnp.float32)
    return lax.linalg.triangular_solve(lower, identity, left_side=True, lower=True).T


def per_device(panels, closure_cols):
    local_rows = panels.shape[0]
    half_width = panels.shape[2]
    width = 2 * half_width
    block_count = local_rows // B
    device_row = lax.axis_index("rows")
    core_index = lax.axis_index("cols")
    gathered = lax.all_gather(panels, "cols", axis=2, tiled=True)
    block_ids = device_row * block_count + jnp.arange(block_count)
    column_ids = jnp.arange(2 * S)
    touched = jnp.any(closure_cols[:, :, None] == column_ids[None, None, :], axis=1)
    in_first = block_ids < S
    in_second = (block_ids >= R) & (block_ids < R + S)
    present = jnp.where(
        in_first[:, None], column_ids[None, :] < S, jnp.where(in_second[:, None], True, touched)
    )
    present = present.astype(jnp.float32)
    kept = gathered.reshape(block_count, B, 2, S, B) * present.reshape(block_count, 1, 2, S, 1)
    kept = kept.reshape(local_rows, 2, width)
    first = kept[:, 0, :]
    second = kept[:, 1, :]

    def own_columns(matrix):
        return lax.dynamic_slice_in_dim(matrix, core_index * half_width, half_width, 1)

    lead_block = broadcast(first, "rows", 0)
    second_rows = (broadcast(first, "rows", 1), broadcast(second, "rows", 1))
    inverse_one = upper_inverse(lead_block)
    one_own = product(first, own_columns(inverse_one))
    one_whole = lax.all_gather(one_own, "cols", axis=1, tiled=True)
    lower_left = product(second_rows[0], inverse_one)
    schur_block = second_rows[1] - product(lower_left, lower_left.T)
    inverse_two = upper_inverse(schur_block)
    left_part = lax.dynamic_slice_in_dim(lower_left, core_index * half_width, half_width, 0)
    updated_own = own_columns(second) - product(one_whole, left_part.T)
    updated_whole = lax.all_gather(updated_own, "cols", axis=1, tiled=True)
    two_own = product(updated_whole, own_columns(inverse_two))
    keep_rows = jnp.repeat(1.0 - in_first.astype(jnp.float32), B)
    two_own = two_own * keep_rows[:, None]
    return jnp.stack([one_own, two_own], axis=1)


def solution(mesh):
    in_specs = (P("rows", None, "cols"), P("rows", None))
    out_specs = P("rows", None, "cols")
    return jax.shard_map(
        per_device, mesh=mesh, in_specs=in_specs, out_specs=out_specs, check_vma=False
    )
```

profile of v0, /device:TPU:29, one launch (start us, length us, event | category | flops | bytes accessed | tf_op | source)
XLA Modules:
  0.0 811.4 jit_solution(10736043606368677142)
XLA Ops:
  16.0 7.6 mul.32
  40.3 225.3 %all-reduce.4.cloned.1.call-done = (f32[768,768]{0,1:T(8,128)}, f32[768,768]{0,1:T(8,128)}, f32[768,768]{0,1:T(8,128)}) async-done(((f32[768,768]{0,1:T(8,128)}, f32[768,768]{0,1:T(8,128)}, f32[768,768]{0,1:T(8,128)}), (f32[768,768]{0,1:T(8,128)}, f32[768,768]{0,1:T(8,128)}, f32[768,768]{0,1:T(8,128)})) %all-reduce.4.cloned.1.call-update) | async-done | bytes 7077904 | tf_op jit(solution)/shard_map/psum | solution.py:13
  272.6 11.7 %cholesky.453 = f32[128,128]{1,0:T(8,128)S(1)} custom-call(f32[128,128]{1,0:T(8,128)S(1)} %cholesky.669), custom_call_target="Cholesky" | custom-call | tf_op jit(solution)/shard_map/jit(cholesky)/cholesky | solution.py:21
  284.3 9.8 %custom-call.41 = f32[1,128,128]{1,2,0:T(8,128)S(1)} custom-call(f32[1,128,128]{2,1,0:T(8,128)S(1)} %get-tuple-element.101), custom_call_target="InvertDiagBlocksLowerTriangular" | custom-call | tf_op jit(solution)/shard_map/jit(cholesky)/cholesky | solution.py:21
  297.1 11.7 %cholesky.472 = f32[128,128]{1,0:T(8,128)S(1)} custom-call(f32[128,128]{1,0:T(8,128)S(1)} %cholesky.673), custom_call_target="Cholesky" | custom-call | tf_op jit(solution)/shard_map/jit(cholesky)/cholesky | solution.py:21
  310.2 10.3 %custom-call.42 = f32[1,128,128]{1,2,0:T(8,128)S(1)} custom-call(f32[1,128,128]{2,1,0:T(8,128)S(1)} %get-tuple-element.98), custom_call_target="InvertDiagBlocksLowerTriangular" | custom-call | tf_op jit(solution)/shard_map/jit(cholesky)/cholesky | solution.py:21
  322.4 11.7 %cholesky.493 = f32[128,128]{1,0:T(8,128)S(1)} custom-call(f32[128,128]{1,0:T(8,128)S(1)} %cholesky.678), custom_call_target="Cholesky" | custom-call | tf_op jit(solution)/shard_map/jit(cholesky)/cholesky | solution.py:21
  334.8 9.8 %custom-call.43 = f32[1,128,128]{1,2,0:T(8,128)S(1)} custom-call(f32[1,128,128]{2,1,0:T(8,128)S(1)} %get-tuple-element.95), custom_call_target="InvertDiagBlocksLowerTriangular" | custom-call | tf_op jit(solution)/shard_map/jit(cholesky)/cholesky | solution.py:21
  346.5 11.9 %cholesky.512 = f32[128,128]{1,0:T(8,128)S(1)} custom-call(f32[128,128]{1,0:T(8,128)S(1)} %cholesky.683), custom_call_target="Cholesky" | custom-call | tf_op jit(solution)/shard_map/jit(cholesky)/cholesky | solution.py:21
  359.1 9.8 %custom-call.44 = f32[1,128,128]{1,2,0:T(8,128)S(1)} custom-call(f32[1,128,128]{2,1,0:T(8,128)S(1)} %get-tuple-element.92), custom_call_target="InvertDiagBlocksLowerTriangular" | custom-call | tf_op jit(solution)/shard_map/jit(cholesky)/cholesky | solution.py:21
  370.7 11.7 %cholesky.531 = f32[128,128]{1,0:T(8,128)S(1)} custom-call(f32[128,128]{1,0:T(8,128)S(1)} %cholesky.688), custom_call_target="Cholesky" | custom-call | tf_op jit(solution)/shard_map/jit(cholesky)/cholesky | solution.py:21
  383.1 9.8 %custom-call.45 = f32[1,128,128]{1,2,0:T(8,128)S(1)} custom-call(f32[1,128,128]{2,1,0:T(8,128)S(1)} %get-tuple-element.89), custom_call_target="InvertDiagBlocksLowerTriangular" | custom-call | tf_op jit(solution)/shard_map/jit(cholesky)/cholesky | solution.py:21
  394.5 12.1 %cholesky.548 = f32[128,128]{1,0:T(8,128)S(1)} custom-call(f32[128,128]{1,0:T(8,128)S(1)} %convolution_subtract_fusion.19), custom_call_target="Cholesky" | custom-call | tf_op jit(solution)/shard_map/jit(cholesky)/cholesky | solution.py:21
  412.7 17.5 %while.4 = (s32[]{:T(128)}, f32[768,768]{1,0:T(8,128)}, s32[6,2]{0,1:T(2,128)S(1)}, f32[6,128,128]{2,1,0:T(8,128)S(1)}, s32[]{:T(128)}) while((s32[]{:T(128)}, f32[768,768]{1,0:T(8,128)}, s32[6,2]{0,1:T(2,128)S(1)}, f32[6,128,128]{2,1,0:T(8,128)S(1)}, s32[]{:T(128)}) %tuple.79), condition=%wide.while_cond, body=%wide.while_body.sunk | while | flops 2 | bytes 131181 | solution.py:23
  430.2 59.0 %custom-call.46 = f32[6,128,128]{1,2,0:T(8,128)S(1)} custom-call(f32[6,128,128]{2,1,0:T(8,128)S(1)} %get-tuple-element.21), custom_call_target="InvertDiagBlocksLowerTriangular" | custom-call | tf_op jit(solution)/shard_map/triangular_solve/custom-call.5 | solution.py:23
  502.6 11.7 %fusion.124 = f32[768,768]{1,0:T(8,128)S(1)} fusion(f32[768,768]{0,1:T(8,128)S(1)} %copy-done.9, f32[768,768]{1,0:T(8,128)S(1)} %convolution_dynamic-update-slice_fusion.1), kind=kOutput, calls=%fused_computation.251 | convolution fusion | flops 5435817984 | bytes 7077888 | tf_op jit(solution)/shard_map/dot_general | solution.py:17
  514.3 7.4 convolution_subtract_fusion
  529.2 11.7 %cholesky.563 = f32[128,128]{1,0:T(8,128)S(1)} custom-call(f32[128,128]{1,0:T(8,128)S(1)} %cholesky.692), custom_call_target="Cholesky" | custom-call | tf_op jit(solution)/shard_map/jit(cholesky)/cholesky | solution.py:21
  542.5 9.8 %custom-call.47 = f32[1,128,128]{1,2,0:T(8,128)S(1)} custom-call(f32[1,128,128]{2,1,0:T(8,128)S(1)} %get-tuple-element.85), custom_call_target="InvertDiagBlocksLowerTriangular" | custom-call | tf_op jit(solution)/shard_map/jit(cholesky)/cholesky | solution.py:21
  555.8 11.7 %cholesky.582 = f32[128,128]{1,0:T(8,128)S(1)} custom-call(f32[128,128]{1,0:T(8,128)S(1)} %cholesky.696), custom_call_target="Cholesky" | custom-call | tf_op jit(solution)/shard_map/jit(cholesky)/cholesky | solution.py:21
  569.5 10.2 %custom-call.48 = f32[1,128,128]{1,2,0:T(8,128)S(1)} custom-call(f32[1,128,128]{2,1,0:T(8,128)S(1)} %get-tuple-element.82), custom_call_target="InvertDiagBlocksLowerTriangular" | custom-call | tf_op jit(solution)/shard_map/jit(cholesky)/cholesky | solution.py:21
  582.5 11.7 %cholesky.603 = f32[128,128]{1,0:T(8,128)S(1)} custom-call(f32[128,128]{1,0:T(8,128)S(1)} %cholesky.701), custom_call_target="Cholesky" | custom-call | tf_op jit(solution)/shard_map/jit(cholesky)/cholesky | solution.py:21
  595.6 9.8 %custom-call.49 = f32[1,128,128]{1,2,0:T(8,128)S(1)} custom-call(f32[1,128,128]{2,1,0:T(8,128)S(1)} %get-tuple-element.79), custom_call_target="InvertDiagBlocksLowerTriangular" | custom-call | tf_op jit(solution)/shard_map/jit(cholesky)/cholesky | solution.py:21
  608.3 11.8 %cholesky.622 = f32[128,128]{1,0:T(8,128)S(1)} custom-call(f32[128,128]{1,0:T(8,128)S(1)} %cholesky.706), custom_call_target="Cholesky" | custom-call | tf_op jit(solution)/shard_map/jit(cholesky)/cholesky | solution.py:21
  621.5 9.8 %custom-call.50 = f32[1,128,128]{1,2,0:T(8,128)S(1)} custom-call(f32[1,128,128]{2,1,0:T(8,128)S(1)} %get-tuple-element.76), custom_call_target="InvertDiagBlocksLowerTriangular" | custom-call | tf_op jit(solution)/shard_map/jit(cholesky)/cholesky | solution.py:21
  634.0 11.7 %cholesky.641 = f32[128,128]{1,0:T(8,128)S(1)} custom-call(f32[128,128]{1,0:T(8,128)S(1)} %cholesky.711), custom_call_target="Cholesky" | custom-call | tf_op jit(solution)/shard_map/jit(cholesky)/cholesky | solution.py:21
  647.0 9.8 %custom-call.51 = f32[1,128,128]{1,2,0:T(8,128)S(1)} custom-call(f32[1,128,128]{2,1,0:T(8,128)S(1)} %get-tuple-element.73), custom_call_target="InvertDiagBlocksLowerTriangular" | custom-call | tf_op jit(solution)/shard_map/jit(cholesky)/cholesky | solution.py:21
  659.3 11.9 %cholesky.658 = f32[128,128]{1,0:T(8,128)S(1)} custom-call(f32[128,128]{1,0:T(8,128)S(1)} %convolution_subtract_fusion.18), custom_call_target="Cholesky" | custom-call | tf_op jit(solution)/shard_map/jit(cholesky)/cholesky | solution.py:21
  672.5 10.5 %fusion.4 = f32[768,384]{1,0:T(8,128)} fusion(f32[768,2,768]{0,2,1:T(8,128)} %copy-done, f32[768,768]{1,0:T(8,128)} %copy-done.5, s32[]{:T(128)S(6)} %select_n.52), kind=kOutput, calls=%fused_computation.17 | convolution fusion | flops 2717908992 | bytes 4718596 | tf_op jit(solution)/shard_map/dot_general | solution.py:17
  690.1 17.0 %while.5 = (s32[]{:T(128)}, f32[768,768]{1,0:T(8,128)}, s32[6,2]{0,1:T(2,128)S(1)}, f32[6,128,128]{2,1,0:T(8,128)S(1)}, s32[]{:T(128)}) while((s32[]{:T(128)}, f32[768,768]{1,0:T(8,128)}, s32[6,2]{0,1:T(2,128)S(1)}, f32[6,128,128]{2,1,0:T(8,128)S(1)}, s32[]{:T(128)}) %tuple.94), condition=%wide.while_cond.clone, body=%wide.while_body.clone.sunk | while | flops 2 | bytes 131181 | solution.py:23
  707.1 59.4 %custom-call.52 = f32[6,128,128]{1,2,0:T(8,128)S(1)} custom-call(f32[6,128,128]{2,1,0:T(8,128)S(1)} %get-tuple-element.22), custom_call_target="InvertDiagBlocksLowerTriangular" | custom-call | tf_op jit(solution)/shard_map/triangular_solve/custom-call.5 | solution.py:23
  791.4 9.8 %fusion.22 = f32[768,1,384]{2,0,1:T(8,128)S(1)} fusion(f32[768,768]{0,1:T(8,128)} %all-gather.8.cloned.1.call-done, f32[768,768]{1,0:T(8,128)} %convolution_dynamic-update-slice_fusion, s32[]{:T(128)S(6)} %select_n.52, f32[768]{0:T(1024)S(1)} %mul.35), kind=kOutput, calls=%fused_computation.38 | convolution fusion | flops 2718203904 | bytes 4721668 | tf_op jit(solution)/shard_map/dot_general | solution.py:17
  (177 shorter events, 158.9 us)
Async XLA Ops:
  6.5 21.6 %all-gather.4.cloned.1.call-start = ((), (), s32[]{:S(2)}) async-start(), calls=%async_computation | async-start | bytes 7077888 | tf_op jit(solution)/shard_map/all_gather | solution.py:33
  11.8 0.7 copy-start.11
  11.9 253.7 %all-reduce.4.cloned.1.call-start = ((), (), s32[]{:S(2)}) async-start(), calls=%async_computation.3 | async-start | bytes 14155776 | tf_op jit(solution)/shard_map/psum | solution.py:13
  32.5 3.6 copy-start
  38.5 730.4 %all-gather.6.cloned.1.call-start = ((), (), s32[]{:S(2)}) async-start(), calls=%async_computation.1 | async-start | bytes 3538944 | tf_op jit(solution)/shard_map/all_gather | solution.py:55
  265.6 3.5 copy-start.4
  271.0 1.5 copy-start.6
  430.2 62.6 %copy-start.1 = (f32[768,768]{1,0:T(8,128)S(1)}, f32[768,768]{1,0:T(8,128)}, u32[]{:S(2)}) copy-start(f32[768,768]{1,0:T(8,128)} %fusion.2) | copy-start | bytes 7077892
  499.1 3.5 copy-start.9
  502.6 11.7 %copy-start.5 = (f32[768,768]{1,0:T(8,128)}, f32[768,768]{1,0:T(8,128)S(1)}, u32[]{:S(2)}) copy-start(f32[768,768]{1,0:T(8,128)S(1)} %convolution_dynamic-update-slice_fusion.1) | copy-start | bytes 7077892
  502.6 11.7 %copy-start.10 = (f32[768,768]{0,1:T(8,128)S(1)}, f32[768,768]{0,1:T(8,128)}, u32[]{:S(2)}) copy-start(f32[768,768]{0,1:T(8,128)} %get-tuple-element.41) | copy-start | bytes 7077892
  527.7 1.5 copy-start.7
  683.0 108.3 %all-gather.8.cloned.1.call-start = ((), (), s32[]{:S(2)}) async-start(), calls=%async_computation.2 | async-start | bytes 3538944 | tf_op jit(solution)/shard_map/all_gather | solution.py:61
  775.0 3.1 copy-start.2
  784.3 2.1 copy-start.8
  791.4 9.8 %copy-start.3 = (f32[768,384]{1,0:T(8,128)S(1)}, f32[768,384]{1,0:T(8,128)}, u32[]{:S(2)}) copy-start(f32[768,384]{1,0:T(8,128)} %fusion.4) | copy-start | bytes 3538948
Sparse Core Ops, SparseCore 0:
  12.0 16.0 all-gather.3
  38.6 226.8 all-reduce.3
  683.1 12.4 all-gather.5
  775.1 12.5 all-gather.7
where the time goes:
time: 820 us; the launch traced here: 811 us
  other arithmetic  391 us (48%)
  waiting for transfers between devices  230 us (28%)
  matrix products  102 us (12%)
  local copies, waits for them, and re-layouts  66.8 us (8%)
  between operations  21.4 us (3%)
    another operation x46, other arithmetic, upper_inverse(): lower = jnp.linalg.cholesky(matrix)  252 us
    psum x1, waiting for transfers between devices, broadcast(): return lax.psum(block, axis)  225 us
    another operation x5, other arithmetic, upper_inverse(): lax.linalg.triangular_solve(lower, identity, left_side=True, lower=True)  123 us
    dot_general x5, matrix products, product(): jnp.dot(left, right, precision=lax.Precision.HIGHEST, preferred_element_t...  45.4 us
    another operation x39, local copies, waits for them, and re-layouts, upper_inverse(): lax.linalg.triangular_solve(lower, identity, left_side=True, lower=True)  34.3 us
    another operation x22, matrix products, upper_inverse(): lax.linalg.triangular_solve(lower, identity, left_side=True, lower=True)  32.1 us
    another operation x20, matrix products, upper_inverse(): lower = jnp.linalg.cholesky(matrix)  24.2 us
  transfers between devices with their start and end apart: 4, of which 2 were waited for; matrix products, arithmetic and copies ran while one was open for 14% of the time, Pallas kernels for 0%

commit v1 on v0

v1 whole, which is shorter than its diff:
```python
import functools

import jax
import jax.numpy as jnp
from jax import lax
from jax.experimental import pallas as pl
from jax.experimental.pallas import tpu as pltpu
from jax.sharding import PartitionSpec as P

B = 96
S = 8
R = 8
G = 8
T = 128
NT = (((1,), (1,)), ((), ()))


def broadcast(block, axis, holder):
    block = jnp.where(lax.axis_index(axis) == holder, block, jnp.zeros_like(block))
    return lax.psum(block, axis)


def dot_nt(left, right, precision=lax.Precision.HIGHEST):
    return lax.dot_general(left, right, NT, precision=precision, preferred_element_type=jnp.float32)


def lanes(x, j):
    return jnp.broadcast_to(x[:, j:j + 1], (G, T))


def subs(x, i):
    return jnp.broadcast_to(x[i:i + 1, :], (G, T))


def invert_factor(groups):
    count = T // G
    row = lax.broadcasted_iota(jnp.int32, (G, T), 0)
    col = lax.broadcasted_iota(jnp.int32, (G, T), 1)
    a = list(groups)
    x = [jnp.where(col == row + G * g, 1.0, 0.0).astype(jnp.float32) for g in range(count)]
    out = []
    for p in range(count):
        columns = [lanes(a[p], G * p + k) for k in range(G)]
        s = [[subs(columns[k], i) for k in range(G)] for i in range(G)]
        wa = [subs(a[p], i) for i in range(G)]
        wx = [subs(x[p], i) for i in range(G)]
        fx = list(wx)
        pivots = []
        for k in range(G):
            inv = 1.0 / s[k][k]
            pivots.append(s[k][k])
            scaled = [None] * G
            for j in range(k + 1, G):
                scaled[j] = s[k][j] * inv
            wa[k] = wa[k] * inv
            wx[k] = wx[k] * inv
            low = fx[k] * inv
            for i in range(G):
                if i == k:
                    continue
                for j in range(k + 1, G):
                    s[i][j] = s[i][j] - s[i][k] * scaled[j]
                wa[i] = wa[i] - s[i][k] * wa[k]
                wx[i] = wx[i] - s[i][k] * wx[k]
                if i > k:
                    fx[i] = fx[i] - s[i][k] * low
            for j in range(k + 1, G):
                s[k][j] = scaled[j]
        done = jnp.zeros((G, T), jnp.float32)
        for k in range(G):
            done = jnp.where(row == k, fx[k] * lax.rsqrt(pivots[k]), done)
        out.append(done)
        for g in range(p + 1, count):
            mult = [lanes(a[g], G * p + k) for k in range(G)]
            pa = [mult[k] * wa[k] for k in range(G)]
            px = [mult[k] * wx[k] for k in range(G)]
            while len(pa) > 1:
                pa = [pa[q] + pa[q + 1] for q in range(0, len(pa), 2)]
                px = [px[q] + px[q + 1] for q in range(0, len(px), 2)]
            a[g] = a[g] - pa[0]
            x[g] = x[g] - px[0]
    return out


def factor_kernel(m_ref, x_ref, y_ref, z, t_ref):
    n = m_ref.shape[0]
    extra = x_ref.shape[0]
    total = n + extra
    blocks = n // T
    chunk = 3 * T
    z[:n, :] = m_ref[...]
    z[n:, :] = x_ref[...]

    def step(b, carry):
        here = pl.ds(pl.multiple_of(b * T, T), T)
        block = z[here, here]
        rows = invert_factor([block[G * g:G * (g + 1), :] for g in range(T // G)])
        for g in range(T // G):
            t_ref[G * g:G * (g + 1), :] = rows[g]
        inverse = t_ref[...]

        def scale(c, carry):
            at = pl.ds(pl.multiple_of(c * chunk, chunk), chunk)
            z[at, here] = dot_nt(z[at, here], inverse)
            return carry

        lax.fori_loop((b + 1) // 3, total // chunk, scale, 0)

        def column(j, carry):
            there = pl.ds(pl.multiple_of(j * T, T), T)
            right = z[there, here]

            def update(c, carry):
                at = pl.ds(pl.multiple_of(c * chunk, chunk), chunk)
                z[at, there] = z[at, there] - dot_nt(z[at, here], right)
                return carry

            lax.fori_loop(j // 3, total // chunk, update, 0)
            return carry

        lax.fori_loop(b + 1, blocks, column, 0)
        return carry

    lax.fori_loop(0, blocks, step, 0)
    y_ref[...] = z[n:, :]


def per_device(cols, panels, closure_cols):
    local_rows = panels.shape[0]
    half_width = panels.shape[2]
    width = cols * half_width
    block_count = local_rows // B
    device_row = lax.axis_index("rows")
    core_index = lax.axis_index("cols")
    gathered = lax.all_gather(panels, "cols", axis=2, tiled=True)
    block_ids = device_row * block_count + jnp.arange(block_count)
    column_ids = jnp.arange(2 * S)
    touched = jnp.any(closure_cols[:, :, None] == column_ids[None, None, :], axis=1)
    in_first = block_ids < S
    in_second = (block_ids >= R) & (block_ids < R + S)
    present = jnp.where(
        in_first[:, None], column_ids[None, :] < S, jnp.where(in_second[:, None], True, touched)
    )
    present = present.astype(jnp.float32)
    kept = gathered.reshape(block_count, B, 2, S, B) * present.reshape(block_count, 1, 2, S, 1)
    kept = kept.reshape(local_rows, 2 * width)
    lead = broadcast(kept[:, :width], "rows", 0)
    low = broadcast(kept, "rows", 1)
    matrix = jnp.concatenate(
        [jnp.concatenate([lead, jnp.zeros_like(lead)], axis=1), low], axis=0
    )
    share = local_rows // cols
    mine = lax.dynamic_slice_in_dim(kept, core_index * share, share, 0)
    n = 2 * width
    result = pl.pallas_call(
        factor_kernel,
        out_shape=jax.ShapeDtypeStruct((share, n), jnp.float32),
        in_specs=[pl.BlockSpec(memory_space=pltpu.VMEM)] * 2,
        out_specs=pl.BlockSpec(memory_space=pltpu.VMEM),
        scratch_shapes=[
            pltpu.VMEM((n + share, n), jnp.float32),
            pltpu.VMEM((T, T), jnp.float32),
        ],
        compiler_params=pltpu.CompilerParams(vmem_limit_bytes=48 * 1024 * 1024),
    )(matrix, mine)
    keep_rows = jnp.repeat(1.0 - in_first.astype(jnp.float32), B)
    keep_mine = lax.dynamic_slice_in_dim(keep_rows, core_index * share, share, 0)
    result = result.reshape(share, 2, width)
    result = result * jnp.stack([jnp.ones_like(keep_mine), keep_mine], axis=1)[:, :, None]
    return lax.all_to_all(result, "cols", split_axis=2, concat_axis=0, tiled=True)


def solution(mesh):
    in_specs = (P("rows", None, "cols"), P("rows", None))
    out_specs = P("rows", None, "cols")
    return jax.shard_map(
        functools.partial(per_device, mesh.shape["cols"]),
        mesh=mesh, in_specs=in_specs, out_specs=out_specs, check_vma=False,
    )
```

time: 820 us -> 433 us (0.53)
  other arithmetic: 391 us -> 12.8 us
  Pallas kernels: 0 us -> 134 us
  matrix products: 102 us -> 0 us
  local copies, waits for them, and re-layouts: 66.8 us -> 32.7 us
    another operation x52 -> x0, other arithmetic: 375 us -> none  [the longest x46 252 us: upper_inverse(): lower = jnp.linalg.cholesky(matrix)]
    pallas_call x0 -> x1, Pallas kernels: none -> 134 us  [per_device(): pl.pallas_call(factor_kernel, out_shape=jax.ShapeDtypeStruct((share, n),...]
    another operation x42 -> x0, matrix products: 56.3 us -> none  [the longest x22 32.1 us: upper_inverse(): lax.linalg.triangular_solve(lower, identity, left_side=True, lower=True)]
    dot_general x5 -> x0, matrix products: 45.4 us -> none  [product(): jnp.dot(left, right, precision=lax.Precision.HIGHEST, preferred_element_t...]
    another operation x52 -> x2, local copies, waits for them, and re-layouts: 39.3 us -> 0.02 us  [per_device(): jnp.stack([jnp.ones_like(keep_mine), keep_mine], axis=1)[:, :, None]]
  transfers between devices with their start and end apart: 4 -> 2, of which waited for: 2 -> 2; matrix products, arithmetic and copies ran while one was open for 14% -> 3% of each run, Pallas kernels for 0% -> 0%
where the time goes in v1:
time: 433 us; the launch traced here: 429 us
  waiting for transfers between devices  230 us (53%)
  Pallas kernels  134 us (31%)
  local copies, waits for them, and re-layouts  32.7 us (8%)
  between operations  13.5 us (3%)
  other arithmetic  12.8 us (3%)
  blocking collectives  5.75 us (1%)
    psum x1, waiting for transfers between devices, broadcast(): return lax.psum(block, axis)  224 us
    pallas_call x1, Pallas kernels, per_device(): pl.pallas_call(factor_kernel, out_shape=jax.ShapeDtypeStruct((share, n),...  134 us
    mul x2, local copies, waits for them, and re-layouts, per_device(): gathered.reshape(block_count, B, 2, S, B)  11.1 us
  transfers between devices with their start and end apart: 2, of which 2 were waited for; matrix products, arithmetic and copies ran while one was open for 3% of the time, Pallas kernels for 0%

profile of v1, /device:TPU:29, one launch (start us, length us, event | category | flops | bytes accessed | tf_op | source)
XLA Modules:
  0.0 428.7 jit_solution(14788897188922073755)
XLA Ops:
  6.5 0.0 all-gather.2.cloned.1.call-start
  6.5 0.7 all-gather.2.cloned.1.call-update
  7.3 0.0 all-reduce.5.cloned.1.call-start
  7.3 0.8 copy.15
  8.1 0.1 fusion
  8.2 0.1 copy.16
  8.3 0.1 fusion.2
  8.4 0.1 copy.17
  8.4 3.1 mul.27
  11.6 8.0 %mul.28 = f32[768,1536]{1,0:T(8,128)} reshape(f32[8,96,2,8,96]{4,3,2,1,0:T(8,128)} %mul.27) | data formatting | bytes 9437184 | tf_op jit(solution)/shard_map/mul | solution.py:145
  19.5 4.7 %all-gather.2.cloned.1.call-done = f32[768,2,768]{2,1,0:T(2,128)} async-done(((f32[768,2,384]{2,1,0:T(2,128)}), f32[768,2,768]{2,1,0:T(2,128)}) %all-gather.2.cloned.1.call-update) | async-done | bytes 4718608 | tf_op jit(solution)/shard_map/all_gather | solution.py:135
  24.2 2.8 copy.20
  27.1 0.9 copy-done.2
  28.0 3.2 broadcast_select_fusion
  31.2 0.0 copy-start.1
  31.2 2.2 copy-done.1
  33.3 1.6 slice_select_fusion
  35.0 0.0 all-reduce.5.cloned.1.call-update
  35.0 0.1 broadcast_in_dim.45
  35.1 0.1 reshape.58
  35.1 0.1 dynamic_slice.7
  35.2 1.8 constant_dynamic-slice_fusion.x_ref
  37.1 224.2 %all-reduce.5.cloned.1.call-done = (f32[768,768]{1,0:T(8,128)}, f32[768,1536]{1,0:T(8,128)}) async-done(((f32[768,768]{1,0:T(8,128)}, f32[768,1536]{1,0:T(8,128)}), (f32[768,768]{1,0:T(8,128)}, f32[768,1536]{1,0:T(8,128)})) %all-reduce.5.cloned.1.call-update) | async-done | bytes 7077904 | tf_op jit(solution)/shard_map/psum | solution.py:20
  261.3 7.7 %select_maximum_fusion.m_ref = f32[1536,1536]{1,0:T(8,128)} fusion(f32[768,768]{1,0:T(8,128)} %get-tuple-element.5, f32[768,1536]{1,0:T(8,128)} %get-tuple-element.6), kind=kLoop, calls=%fused_computation | loop fusion | flops 7077888 | bytes 16515072 | tf_op jit(solution)/shard_map/concatenate | solution.py:149
  269.0 134.3 %shard_map.28 = f32[384,1536]{1,0:T(8,128)S(1)} custom-call(f32[1536,1536]{1,0:T(8,128)} %select_maximum_fusion.m_ref, f32[384,1536]{1,0:T(8,128)S(1)} %constant_dynamic-slice_fusion.x_ref), custom_call_target="tpu_custom_call" | custom-call | tf_op jit(solution)/shard_map/pallas_call | solution.py:155
  403.2 0.0 copy-start
  403.3 1.4 copy-done
  404.7 3.9 reshape.57
  408.6 3.9 copy.18
  412.5 0.2 broadcast_multiply_fusion
  412.7 5.8 %all_to_all.18 = f32[384,2,768]{0,1,2:T(2,128)S(1)} all-to-all(f32[384,2,768]{0,1,2:T(2,128)S(1)} %bitcast.19), channel_id=1, replica_groups=mesh['rows'=16,'cols'=2] {'cols'}, dimensions={2} | all-to-all | bytes 4718592 | tf_op jit(solution)/shard_map/all_to_all | solution.py:170
  418.4 3.5 copy.19
  (7 shorter events, 0.0 us)
Async XLA Ops:
  6.5 17.7 %all-gather.2.cloned.1.call-start = ((), (), s32[]{:S(2)}) async-start(), calls=%async_computation.1 | async-start | bytes 7077888 | tf_op jit(solution)/shard_map/all_gather | solution.py:135
  7.3 254.1 %all-reduce.5.cloned.1.call-start = ((), (), s32[]{:S(2)}) async-start(), calls=%async_computation.2 | async-start | bytes 14155776 | tf_op jit(solution)/shard_map/psum | solution.py:20
  24.2 3.8 copy-start.2
  31.2 2.2 copy-start.1
  403.2 1.4 copy-start
Sparse Core Ops, SparseCore 0:
  8.9 15.2 all-gather.1
  35.1 226.1 all-reduce.4

commit v2 on v1

v2 whole, which is shorter than its diff:
```python
import functools

import jax
import jax.numpy as jnp
from jax import lax
from jax.experimental import pallas as pl
from jax.experimental.pallas import tpu as pltpu
from jax.sharding import PartitionSpec as P

B = 96
S = 8
R = 8
G = 8
T = 128
NT = (((1,), (1,)), ((), ()))


def dot_nt(left, right, precision=lax.Precision.HIGHEST):
    return lax.dot_general(left, right, NT, precision=precision, preferred_element_type=jnp.float32)


def lanes(x, j):
    return jnp.broadcast_to(x[:, j:j + 1], (G, T))


def subs(x, i):
    return jnp.broadcast_to(x[i:i + 1, :], (G, T))


def invert_factor(groups):
    count = T // G
    row = lax.broadcasted_iota(jnp.int32, (G, T), 0)
    col = lax.broadcasted_iota(jnp.int32, (G, T), 1)
    a = list(groups)
    x = [jnp.where(col == row + G * g, 1.0, 0.0).astype(jnp.float32) for g in range(count)]
    out = []
    for p in range(count):
        columns = [lanes(a[p], G * p + k) for k in range(G)]
        s = [[subs(columns[k], i) for k in range(G)] for i in range(G)]
        wa = [subs(a[p], i) for i in range(G)]
        wx = [subs(x[p], i) for i in range(G)]
        fx = list(wx)
        pivots = []
        for k in range(G):
            inv = 1.0 / s[k][k]
            pivots.append(s[k][k])
            scaled = [None] * G
            for j in range(k + 1, G):
                scaled[j] = s[k][j] * inv
            wa[k] = wa[k] * inv
            wx[k] = wx[k] * inv
            low = fx[k] * inv
            for i in range(G):
                if i == k:
                    continue
                for j in range(k + 1, G):
                    s[i][j] = s[i][j] - s[i][k] * scaled[j]
                wa[i] = wa[i] - s[i][k] * wa[k]
                wx[i] = wx[i] - s[i][k] * wx[k]
                if i > k:
                    fx[i] = fx[i] - s[i][k] * low
            for j in range(k + 1, G):
                s[k][j] = scaled[j]
        done = jnp.zeros((G, T), jnp.float32)
        for k in range(G):
            done = jnp.where(row == k, fx[k] * lax.rsqrt(pivots[k]), done)
        out.append(done)
        for g in range(p + 1, count):
            mult = [lanes(a[g], G * p + k) for k in range(G)]
            pa = [mult[k] * wa[k] for k in range(G)]
            px = [mult[k] * wx[k] for k in range(G)]
            while len(pa) > 1:
                pa = [pa[q] + pa[q + 1] for q in range(0, len(pa), 2)]
                px = [px[q] + px[q + 1] for q in range(0, len(px), 2)]
            a[g] = a[g] - pa[0]
            x[g] = x[g] - px[0]
    return out


def panel_kernel(counts, p_ref, mask_ref, out_ref, z, t_ref, own_send, own_recv, a_recv, b_recv,
                 a_send, b_send, end_send, end_recv):
    rows, cols = counts
    half = p_ref.shape[2]
    local_rows = p_ref.shape[1]
    width = cols * half
    n = 2 * width
    share = local_rows // cols
    per_half = half // T
    blocks = n // T
    chunk = 3 * T
    r = lax.axis_index("rows")
    c = lax.axis_index("cols")
    other = 1 - c
    q, side = r // 2, r % 2
    pairs = rows // 2
    even = q % 2 == 0
    has_near = jnp.logical_and(even, q + 1 < pairs)
    has_far = jnp.logical_and(even, q + 2 < pairs)
    parent = jnp.where(even, r - 4, r - 2)
    across = jnp.where(side == 0, r + 1, r - 1)

    def to(row, core):
        return dict(device_id=(row, core), device_id_type=pl.DeviceIdType.MESH)

    barrier = pltpu.get_barrier_semaphore()
    pl.semaphore_signal(barrier, inc=1, **to(r, other))
    pl.semaphore_signal(barrier, inc=1, **to(across, c))

    @pl.when(q > 0)
    def _():
        pl.semaphore_signal(barrier, inc=1, **to(parent, c))

    heard = 2 + jnp.where(has_near, 1, 0) + jnp.where(has_far, 1, 0)
    pl.semaphore_wait(barrier, heard)

    def place(kind, k, cc):
        column = cc * per_half + k
        if kind == 0:
            return (0, column * T, width - column * T, k * T), (column * T, column * T)
        if k < per_half:
            return (0, 0, width, k * T), (width, column * T)
        k = k - per_half
        column = cc * per_half + k
        return (1, column * T, width - column * T, k * T), (width + column * T, width + column * T)

    def count(kind):
        return per_half if kind == 0 else 2 * per_half

    recvs, sends = (a_recv, b_recv), (a_send, b_send)

    def copy(kind, k, cc, dest, slot, root):
        (panel, first, length, at), (top, left) = place(kind, k, cc)
        there = z.at[pl.ds(top, length), pl.ds(left, T)]
        source = p_ref.at[panel, pl.ds(first, length), pl.ds(at, T)] if root else there
        return pltpu.make_async_remote_copy(
            src_ref=source, dst_ref=there, send_sem=sends[kind].at[slot, k],
            recv_sem=recvs[kind].at[cc, k], **dest)

    def fan_out(kind, k, cc, root):
        @pl.when(has_far)
        def _():
            copy(kind, k, cc, to(r + 4, c), 0, root).start()

        copy(kind, k, cc, to(across, c), 2, root).start()

        @pl.when(has_near)
        def _():
            copy(kind, k, cc, to(r + 2, c), 1, root).start()

        copy(kind, k, cc, to(r, other), 3, root).start()

    def handle(kind, k, cc):
        @pl.when(jnp.logical_and(side == kind, q == 0))
        def _():
            fan_out(kind, k, cc, True)

        @pl.when(jnp.logical_and(side == kind, q > 0))
        def _():
            copy(kind, k, cc, to(r, other), 3, False).wait_recv()
            fan_out(kind, k, cc, False)

        @pl.when(side != kind)
        def _():
            copy(kind, k, cc, to(r, other), 3, False).wait_recv()
            copy(kind, k, cc, to(r, other), 3, False).start()

    def settle(kind, k, cc):
        @pl.when(side == kind)
        def _():
            @pl.when(has_far)
            def _():
                copy(kind, k, cc, to(r, other), 0, False).wait_send()

            @pl.when(has_near)
            def _():
                copy(kind, k, cc, to(r, other), 1, False).wait_send()

            copy(kind, k, cc, to(r, other), 2, False).wait_send()

        copy(kind, k, cc, to(r, other), 3, False).wait_send()
        copy(kind, k, 1 - cc, to(r, other), 3, False).wait_recv()

    def swap(panel):
        return pltpu.make_async_remote_copy(
            src_ref=p_ref.at[panel, pl.ds(pl.multiple_of(other * share, 8), share), :],
            dst_ref=z.at[pl.ds(n, share), pl.ds(pl.multiple_of(panel * width + c * half, T), half)],
            send_sem=own_send.at[panel], recv_sem=own_recv.at[panel], **to(r, other))

    order = []
    for k in range(per_half):
        order += [(0, k), (1, k)]
    order += [(1, k) for k in range(per_half, 2 * per_half)]
    for cc in range(cols):
        @pl.when(c == cc)
        def _():
            for kind, k in order:
                handle(kind, k, cc)

    for panel in range(2):
        swap(panel).start()
        z[pl.ds(n, share), pl.ds(pl.multiple_of(panel * width + c * half, T), half)] = (
            p_ref[panel, pl.ds(pl.multiple_of(c * share, 8), share), :])

    for cc in range(cols):
        @pl.when(c == cc)
        def _():
            for kind in range(2):
                @pl.when(jnp.logical_and(side == kind, q == 0))
                def _():
                    for k in range(count(kind)):
                        (panel, first, length, at), (top, left) = place(kind, k, cc)
                        z[top:top + length, left:left + T] = p_ref[panel, first:first + length, at:at + T]

            for kind, k in order:
                settle(kind, k, cc)

    for panel in range(2):
        swap(panel).wait()
    group = share // B
    for i in range(group):
        at = slice(n + i * B, n + (i + 1) * B)
        z[at, :] = z[at, :] * mask_ref[pl.ds(c * group + i, 1), :]

    def step(b, carry):
        here = pl.ds(pl.multiple_of(b * T, T), T)
        block = z[here, here]
        done = invert_factor([block[G * g:G * (g + 1), :] for g in range(T // G)])
        for g in range(T // G):
            t_ref[G * g:G * (g + 1), :] = done[g]
        inverse = t_ref[...]

        def scale(i, carry):
            at = pl.ds(pl.multiple_of(i * chunk, chunk), chunk)
            z[at, here] = dot_nt(z[at, here], inverse)
            return carry

        lax.fori_loop((b + 1) // 3, (n + share) // chunk, scale, 0)

        def column(j, carry):
            there = pl.ds(pl.multiple_of(j * T, T), T)
            right = z[there, here]

            def update(i, carry):
                at = pl.ds(pl.multiple_of(i * chunk, chunk), chunk)
                z[at, there] = z[at, there] - dot_nt(z[at, here], right)
                return carry

            lax.fori_loop(j // 3, (n + share) // chunk, update, 0)
            return carry

        lax.fori_loop(b + 1, blocks, column, 0)
        return carry

    lax.fori_loop(0, blocks, step, 0)

    for i in range(group):
        at = slice(n + i * B, n + (i + 1) * B)
        keep = jnp.where(r * (local_rows // B) + c * group + i < S, 0.0, 1.0).astype(jnp.float32)
        z[at, width:] = z[at, width:] * keep

    def finish(panel):
        return pltpu.make_async_remote_copy(
            src_ref=z.at[pl.ds(n, share), pl.ds(pl.multiple_of(panel * width + other * half, T), half)],
            dst_ref=out_ref.at[panel, pl.ds(pl.multiple_of(c * share, 8), share), :],
            send_sem=end_send.at[panel], recv_sem=end_recv.at[panel], **to(r, other))

    for panel in range(2):
        finish(panel).start()
        out_ref[panel, pl.ds(pl.multiple_of(c * share, 8), share), :] = (
            z[pl.ds(n, share), pl.ds(pl.multiple_of(panel * width + c * half, T), half)])
    for panel in range(2):
        finish(panel).wait()


def per_device(counts, panels, closure_cols):
    local_rows = panels.shape[0]
    half = panels.shape[2]
    width = counts[1] * half
    n = 2 * width
    share = local_rows // counts[1]
    per_half = half // T
    block_count = local_rows // B
    block_ids = lax.axis_index("rows") * block_count + jnp.arange(block_count)
    column_ids = jnp.arange(2 * S)
    touched = jnp.any(closure_cols[:, :, None] == column_ids[None, None, :], axis=1)
    in_first = block_ids < S
    in_second = (block_ids >= R) & (block_ids < R + S)
    present = jnp.where(
        in_first[:, None], column_ids[None, :] < S, jnp.where(in_second[:, None], True, touched)
    )
    mask = jnp.repeat(present.astype(jnp.float32), B, axis=1)
    dma = pltpu.SemaphoreType.DMA
    result = pl.pallas_call(
        functools.partial(panel_kernel, counts),
        out_shape=jax.ShapeDtypeStruct((2, local_rows, half), jnp.float32),
        in_specs=[pl.BlockSpec(memory_space=pltpu.VMEM)] * 2,
        out_specs=pl.BlockSpec(memory_space=pltpu.VMEM),
        scratch_shapes=[
            pltpu.VMEM((n + share, n), jnp.float32),
            pltpu.VMEM((T, T), jnp.float32),
            dma((2,)), dma((2,)),
            dma((2, per_half)), dma((2, 2 * per_half)),
            dma((4, per_half)), dma((4, 2 * per_half)),
            dma((2,)), dma((2,)),
        ],
        compiler_params=pltpu.CompilerParams(
            vmem_limit_bytes=48 * 1024 * 1024, collective_id=0, has_side_effects=True
        ),
    )(panels.transpose(1, 0, 2), mask)
    return result.transpose(1, 0, 2)


def solution(mesh):
    in_specs = (P("rows", None, "cols"), P("rows", None))
    out_specs = P("rows", None, "cols")
    counts = (mesh.shape["rows"], mesh.shape["cols"])
    return jax.shard_map(
        functools.partial(per_device, counts),
        mesh=mesh, in_specs=in_specs, out_specs=out_specs, check_vma=False,
    )
```

time: 433 us -> 240 us (0.55)
  waiting for transfers between devices: 230 us -> 0 us
  Pallas kernels: 134 us -> 233 us
  local copies, waits for them, and re-layouts: 32.7 us -> 5.99 us
  between operations: 13.5 us -> 0.03 us
  other arithmetic: 12.8 us -> 0.17 us
  blocking collectives: 5.75 us -> 0 us
    psum x1 -> x0, waiting for transfers between devices: 224 us -> none  [broadcast(): return lax.psum(block, axis)]
    pallas_call x1, Pallas kernels: 134 us -> 233 us  [per_device(): pl.pallas_call(functools.partial(panel_kernel, counts), out_shape=jax.Sha...]
    mul x2 -> x0, local copies, waits for them, and re-layouts: 11.1 us -> none  [per_device(): gathered.reshape(block_count, B, 2, S, B)]
    reshape x3 -> x1, local copies, waits for them, and re-layouts: 7.9 us -> 0.1 us  [per_device(): mask = jnp.repeat(present.astype(jnp.float32), B, axis=1)]
    concatenate x1 -> x0, other arithmetic: 7.66 us -> none  [per_device(): jnp.concatenate([jnp.concatenate([lead, jnp.zeros_like(lead)], axis=1), l...]
    all_to_all x1 -> x0, blocking collectives: 5.75 us -> none  [per_device(): lax.all_to_all(result, 'cols', split_axis=2, concat_axis=0, tiled=True)]
    unnamed x9 -> x2, local copies, waits for them, and re-layouts: 8.09 us -> 2.59 us
    select_n x2 -> x0, other arithmetic: 4.8 us -> none  [broadcast(): jnp.where(lax.axis_index(axis) == holder, block, jnp.zeros_like(block))]
  transfers between devices with their start and end apart: 2 -> 0, of which waited for: 2 -> 0; matrix products, arithmetic and copies ran while one was open for 3% -> 0% of each run, Pallas kernels for 0% -> 0%
where the time goes in v2:
time: 240 us; the launch traced here: 239 us
  Pallas kernels  233 us (97%)
  local copies, waits for them, and re-layouts  5.99 us (2%)
    pallas_call x1, Pallas kernels, per_device(): pl.pallas_call(functools.partial(panel_kernel, counts), out_shape=jax.Sha...  233 us

profile of v2, /device:TPU:29, one launch (start us, length us, event | category | flops | bytes accessed | tf_op | source)
XLA Modules:
  0.0 239.4 jit_solution(4805992882651818345)
XLA Ops:
  0.0 0.8 copy.6
  0.8 0.1 fusion
  0.9 0.1 select_convert_fusion
  1.0 0.1 broadcast_in_dim.40
  1.0 0.1 reshape.19.mask_ref
  1.1 1.8 copy.9
  3.0 233.2 %shard_map.28 = f32[2,768,384]{2,1,0:T(8,128)S(1)} custom-call(f32[2,768,384]{2,1,0:T(8,128)S(1)} %bitcast.5, f32[8,1536]{1,0:T(8,128)S(1)} %reshape.19.mask_ref), custom_call_target="tpu_custom_call" | custom-call | tf_op jit(solution)/shard_map/pallas_call | solution.py:293
  236.2 3.2 %copy.7 = f32[768,2,384]{2,1,0:T(2,128)} copy(f32[768,2,384]{2,0,1:T(8,128)S(1)} %bitcast.4) | data formatting | bytes 4718592 | tf_op jit(solution)/shard_map/transpose | solution.py:310
  (2 shorter events, 0.0 us)

commit v3 on v2

--- a/solution.py
+++ b/solution.py
@@ -32,48 +32,40 @@
     row = lax.broadcasted_iota(jnp.int32, (G, T), 0)
     col = lax.broadcasted_iota(jnp.int32, (G, T), 1)
     a = list(groups)
-    x = [jnp.where(col == row + G * g, 1.0, 0.0).astype(jnp.float32) for g in range(count)]
     out = []
     for p in range(count):
         columns = [lanes(a[p], G * p + k) for k in range(G)]
-        s = [[subs(columns[k], i) for k in range(G)] for i in range(G)]
-        wa = [subs(a[p], i) for i in range(G)]
-        wx = [subs(x[p], i) for i in range(G)]
-        fx = list(wx)
-        pivots = []
+        s = {(i, k): subs(columns[k], i) for k in range(G) for i in range(k + 1)}
+        here = jnp.logical_and(col >= G * p, col < G * (p + 1))
+        unit = jnp.where(col == row + G * p, 1.0, 0.0).astype(jnp.float32)
+        start = jnp.where(here, unit, a[p])
+        w = [subs(start, i) for i in range(G)]
+        inv, m = [], {}
         for k in range(G):
-            inv = 1.0 / s[k][k]
-            pivots.append(s[k][k])
-            scaled = [None] * G
-            for j in range(k + 1, G):
-                scaled[j] = s[k][j] * inv
-            wa[k] = wa[k] * inv
-            wx[k] = wx[k] * inv
-            low = fx[k] * inv
-            for i in range(G):
-                if i == k:
-                    continue
-                for j in range(k + 1, G):
-                    s[i][j] = s[i][j] - s[i][k] * scaled[j]
-                wa[i] = wa[i] - s[i][k] * wa[k]
-                wx[i] = wx[i] - s[i][k] * wx[k]
-                if i > k:
-                    fx[i] = fx[i] - s[i][k] * low
-            for j in range(k + 1, G):
-                s[k][j] = scaled[j]
-        done = jnp.zeros((G, T), jnp.float32)
-        for k in range(G):
-            done = jnp.where(row == k, fx[k] * lax.rsqrt(pivots[k]), done)
-        out.append(done)
+            r = 1.0 / s[k, k]
+            inv.append(r)
+            for i in range(k + 1, G):
+                m[i, k] = s[k, i] * r
+            for i in range(k + 1, G):
+                for j in range(i, G):
+                    s[i, j] = s[i, j] - m[i, k] * s[k, j]
+            for i in range(k + 1, G):
+                w[i] = w[i] - m[i, k] * w[k]
+        done = w[0] * lax.rsqrt(s[0, 0])
+        for k in range(1, G):
+            done = jnp.where(row == k, w[k] * lax.rsqrt(s[k, k]), done)
+        out.append(jnp.where(col < G * (p + 1), done, 0.0))
+        if p == count - 1:
+            break
+        w = [w[k] * inv[k] for k in range(G)]
+        for k in range(G - 1, 0, -1):
+            for i in range(k):
+                w[i] = w[i] - m[k, i] * w[k]
         for g in range(p + 1, count):
-            mult = [lanes(a[g], G * p + k) for k in range(G)]
-            pa = [mult[k] * wa[k] for k in range(G)]
-            px = [mult[k] * wx[k] for k in range(G)]
-            while len(pa) > 1:
-                pa = [pa[q] + pa[q + 1] for q in range(0, len(pa), 2)]
-                px = [px[q] + px[q + 1] for q in range(0, len(px), 2)]
-            a[g] = a[g] - pa[0]
-            x[g] = x[g] - px[0]
+            part = [lanes(a[g], G * p + k) * w[k] for k in range(G)]
+            while len(part) > 1:
+                part = [part[q] + part[q + 1] for q in range(0, len(part), 2)]
+            a[g] = jnp.where(here, 0.0, a[g]) - part[0]
     return out
 
 
@@ -237,18 +229,19 @@
         lax.fori_loop((b + 1) // 3, (n + share) // chunk, scale, 0)
 
         def column(j, carry):
-            there = pl.ds(pl.multiple_of(j * T, T), T)
-            right = z[there, here]
+            there = pl.ds(pl.multiple_of(j * 2 * T, 2 * T), 2 * T)
+            block_row = j * 2 * T + lax.broadcasted_iota(jnp.int32, (2 * T, T), 0)
+            right = jnp.where(block_row >= (b + 1) * T, z[there, here], 0.0)
 
             def update(i, carry):
                 at = pl.ds(pl.multiple_of(i * chunk, chunk), chunk)
                 z[at, there] = z[at, there] - dot_nt(z[at, here], right)
                 return carry
 
-            lax.fori_loop(j // 3, (n + share) // chunk, update, 0)
+            lax.fori_loop(2 * j // 3, (n + share) // chunk, update, 0)
             return carry
 
-        lax.fori_loop(b + 1, blocks, column, 0)
+        lax.fori_loop((b + 1) // 2, blocks // 2, column, 0)
         return carry
 
     lax.fori_loop(0, blocks, step, 0)

time: 240 us -> 231 us (0.963)
  Pallas kernels: 233 us -> 225 us
    pallas_call x1, Pallas kernels: 233 us -> 225 us  [per_device(): pl.pallas_call(functools.partial(panel_kernel, counts), out_shape=jax.Sha...]
where the time goes in v3:
time: 231 us
  Pallas kernels  225 us (97%)
  local copies, waits for them, and re-layouts  5.99 us (3%)
    pallas_call x1, Pallas kernels, per_device(): pl.pallas_call(functools.partial(panel_kernel, counts), out_shape=jax.Sha...  225 us

profile of v3, /device:TPU:29, one launch (start us, length us, event | category | flops | bytes accessed | tf_op | source)
XLA Modules:
  0.0 231.0 jit_solution(10475463803552857839)
XLA Ops:
  0.0 0.8 copy.6
  0.8 0.1 fusion
  0.9 0.1 select_convert_fusion
  1.0 0.1 broadcast_in_dim.40
  1.0 0.1 reshape.19.mask_ref
  1.1 1.8 copy.9
  3.0 224.8 %shard_map.28 = f32[2,768,384]{2,1,0:T(8,128)S(1)} custom-call(f32[2,768,384]{2,1,0:T(8,128)S(1)} %bitcast.5, f32[8,1536]{1,0:T(8,128)S(1)} %reshape.19.mask_ref), custom_call_target="tpu_custom_call" | custom-call | tf_op jit(solution)/shard_map/pallas_call | solution.py:286
  227.8 3.2 %copy.7 = f32[768,2,384]{2,1,0:T(2,128)} copy(f32[768,2,384]{2,0,1:T(8,128)S(1)} %bitcast.4) | data formatting | bytes 4718592 | tf_op jit(solution)/shard_map/transpose | solution.py:303
  (2 shorter events, 0.0 us)

commit v4 on v3

--- a/solution.py
+++ b/solution.py
@@ -27,13 +27,15 @@
     return jnp.broadcast_to(x[i:i + 1, :], (G, T))
 
 
-def invert_factor(groups):
+def invert_factor(groups, between):
     count = T // G
     row = lax.broadcasted_iota(jnp.int32, (G, T), 0)
     col = lax.broadcasted_iota(jnp.int32, (G, T), 1)
     a = list(groups)
     out = []
     for p in range(count):
+        if p in (4, 9, 14):
+            between((4, 9, 14).index(p))
         columns = [lanes(a[p], G * p + k) for k in range(G)]
         s = {(i, k): subs(columns[k], i) for k in range(G) for i in range(k + 1)}
         here = jnp.logical_and(col >= G * p, col < G * (p + 1))
@@ -105,72 +107,79 @@
     heard = 2 + jnp.where(has_near, 1, 0) + jnp.where(has_far, 1, 0)
     pl.semaphore_wait(barrier, heard)
 
-    def place(kind, k, cc):
+    def lead(k, cc, dest, slot, root):
         column = cc * per_half + k
-        if kind == 0:
-            return (0, column * T, width - column * T, k * T), (column * T, column * T)
-        if k < per_half:
-            return (0, 0, width, k * T), (width, column * T)
-        k = k - per_half
-        column = cc * per_half + k
-        return (1, column * T, width - column * T, k * T), (width + column * T, width + column * T)
-
-    def count(kind):
-        return per_half if kind == 0 else 2 * per_half
-
-    recvs, sends = (a_recv, b_recv), (a_send, b_send)
-
-    def copy(kind, k, cc, dest, slot, root):
-        (panel, first, length, at), (top, left) = place(kind, k, cc)
-        there = z.at[pl.ds(top, length), pl.ds(left, T)]
-        source = p_ref.at[panel, pl.ds(first, length), pl.ds(at, T)] if root else there
+        there = z.at[pl.ds(column * T, width - column * T), pl.ds(column * T, T)]
+        near = p_ref.at[0, pl.ds(column * T, width - column * T), pl.ds(k * T, T)]
         return pltpu.make_async_remote_copy(
-            src_ref=source, dst_ref=there, send_sem=sends[kind].at[slot, k],
-            recv_sem=recvs[kind].at[cc, k], **dest)
-
-    def fan_out(kind, k, cc, root):
+            src_ref=near if root else there, dst_ref=there, send_sem=a_send.at[slot, k],
+            recv_sem=a_recv.at[cc, k], **dest)
+
+    part = width // 2
+    pieces = 4 * per_half
+
+    def low(k, core, dest, slot, root):
+        panel, column, piece = k // (2 * per_half), (k % (2 * per_half)) // 2, k % 2
+        there = z.at[
+            pl.ds(pl.multiple_of(width + piece * part, T), part),
+            pl.ds(pl.multiple_of(panel * width + core * half + column * T, T), T)]
+        near = p_ref.at[
+            panel, pl.ds(pl.multiple_of(piece * part, T), part), pl.ds(pl.multiple_of(column * T, T), T)]
+        return pltpu.make_async_remote_copy(
+            src_ref=near if root else there, dst_ref=there, send_sem=b_send.at[slot, k],
+            recv_sem=b_recv.at[core, k], **dest)
+
+    def fan_out(make, k, core, root):
         @pl.when(has_far)
         def _():
-            copy(kind, k, cc, to(r + 4, c), 0, root).start()
-
-        copy(kind, k, cc, to(across, c), 2, root).start()
+            make(k, core, to(r + 4, c), 0, root).start()
+
+        make(k, core, to(across, c), 2, root).start()
 
         @pl.when(has_near)
         def _():
-            copy(kind, k, cc, to(r + 2, c), 1, root).start()
-
-        copy(kind, k, cc, to(r, other), 3, root).start()
-
-    def handle(kind, k, cc):
-        @pl.when(jnp.logical_and(side == kind, q == 0))
-        def _():
-            fan_out(kind, k, cc, True)
-
-        @pl.when(jnp.logical_and(side == kind, q > 0))
-        def _():
-            copy(kind, k, cc, to(r, other), 3, False).wait_recv()
-            fan_out(kind, k, cc, False)
+            make(k, core, to(r + 2, c), 1, root).start()
+
+        make(k, core, to(r, other), 3, root).start()
+
+    def pass_on(make, kind, k, core):
+        make(k, core, to(r, other), 3, False).wait_recv()
+
+        @pl.when(side == kind)
+        def _():
+            fan_out(make, k, core, False)
 
         @pl.when(side != kind)
         def _():
-            copy(kind, k, cc, to(r, other), 3, False).wait_recv()
-            copy(kind, k, cc, to(r, other), 3, False).start()
-
-    def settle(kind, k, cc):
+            make(k, core, to(r, other), 3, False).start()
+
+    def settle(make, kind, k, core, far_core):
         @pl.when(side == kind)
         def _():
             @pl.when(has_far)
             def _():
-                copy(kind, k, cc, to(r, other), 0, False).wait_send()
+                make(k, core, to(r, other), 0, False).wait_send()
 
             @pl.when(has_near)
             def _():
-                copy(kind, k, cc, to(r, other), 1, False).wait_send()
-
-            copy(kind, k, cc, to(r, other), 2, False).wait_send()
-
-        copy(kind, k, cc, to(r, other), 3, False).wait_send()
-        copy(kind, k, 1 - cc, to(r, other), 3, False).wait_recv()
+                make(k, core, to(r, other), 1, False).wait_send()
+
+            make(k, core, to(r, other), 2, False).wait_send()
+
+        make(k, core, to(r, other), 3, False).wait_send()
+        make(k, far_core, to(r, other), 3, False).wait_recv()
+
+    low_source = jnp.logical_and(side == 1, q == 0)
+    lag = (q + 1) // 2 + jnp.where(side == 1, 0, 1)
+
+    def low_turn(t):
+        k = t - lag
+        mine = jnp.logical_and(k >= 0, k < pieces)
+        mine = jnp.logical_and(mine, t < 3 * (blocks // 2))
+
+        @pl.when(jnp.logical_and(jnp.logical_not(low_source), mine))
+        def _():
+            pass_on(low, 1, k, c)
 
     def swap(panel):
         return pltpu.make_async_remote_copy(
@@ -178,15 +187,26 @@
             dst_ref=z.at[pl.ds(n, share), pl.ds(pl.multiple_of(panel * width + c * half, T), half)],
             send_sem=own_send.at[panel], recv_sem=own_recv.at[panel], **to(r, other))
 
-    order = []
-    for k in range(per_half):
-        order += [(0, k), (1, k)]
-    order += [(1, k) for k in range(per_half, 2 * per_half)]
     for cc in range(cols):
         @pl.when(c == cc)
         def _():
-            for kind, k in order:
-                handle(kind, k, cc)
+            @pl.when(jnp.logical_and(side == 0, q == 0))
+            def _():
+                for k in range(per_half):
+                    fan_out(lead, k, cc, True)
+
+            @pl.when(jnp.logical_or(side != 0, q != 0))
+            def _():
+                for k in range(per_half):
+                    pass_on(lead, 0, k, cc)
+
+    @pl.when(low_source)
+    def _():
+        def send(k, carry):
+            fan_out(low, k, c, True)
+            return carry
+
+        lax.fori_loop(0, pieces, send, 0)
 
     for panel in range(2):
         swap(panel).start()
@@ -196,15 +216,17 @@
     for cc in range(cols):
         @pl.when(c == cc)
         def _():
-            for kind in range(2):
-                @pl.when(jnp.logical_and(side == kind, q == 0))
-                def _():
-                    for k in range(count(kind)):
-                        (panel, first, length, at), (top, left) = place(kind, k, cc)
-                        z[top:top + length, left:left + T] = p_ref[panel, first:first + length, at:at + T]
-
-            for kind, k in order:
-                settle(kind, k, cc)
+            @pl.when(jnp.logical_and(side == 0, q == 0))
+            def _():
+                z[:width, cc * half:(cc + 1) * half] = p_ref[0]
+
+            for k in range(per_half):
+                settle(lead, 0, k, cc, 1 - cc)
+
+    @pl.when(low_source)
+    def _():
+        for panel in range(2):
+            z[width:n, pl.ds(pl.multiple_of(panel * width + c * half, T), half)] = p_ref[panel]
 
     for panel in range(2):
         swap(panel).wait()
@@ -213,20 +235,18 @@
         at = slice(n + i * B, n + (i + 1) * B)
         z[at, :] = z[at, :] * mask_ref[pl.ds(c * group + i, 1), :]
 
-    def step(b, carry):
-        here = pl.ds(pl.multiple_of(b * T, T), T)
-        block = z[here, here]
-        done = invert_factor([block[G * g:G * (g + 1), :] for g in range(T // G)])
-        for g in range(T // G):
-            t_ref[G * g:G * (g + 1), :] = done[g]
-        inverse = t_ref[...]
-
+    lead_chunks, n_chunks, end_chunks = width // chunk, n // chunk, (n + share) // chunk
+
+    def scale_rows(here, inverse, first, last):
         def scale(i, carry):
             at = pl.ds(pl.multiple_of(i * chunk, chunk), chunk)
             z[at, here] = dot_nt(z[at, here], inverse)
             return carry
 
-        lax.fori_loop((b + 1) // 3, (n + share) // chunk, scale, 0)
+        lax.fori_loop(first, last, scale, 0)
+
+    def update_rows(b, stop, ranges):
+        here = pl.ds(pl.multiple_of(b * T, T), T)
 
         def column(j, carry):
             there = pl.ds(pl.multiple_of(j * 2 * T, 2 * T), 2 * T)
@@ -238,13 +258,79 @@
                 z[at, there] = z[at, there] - dot_nt(z[at, here], right)
                 return carry
 
-            lax.fori_loop(2 * j // 3, (n + share) // chunk, update, 0)
+            for first, last, lower in ranges:
+                begin = jnp.maximum(first, 2 * j // 3) if lower else first
+                lax.fori_loop(begin, last, update, 0)
             return carry
 
-        lax.fori_loop((b + 1) // 2, blocks // 2, column, 0)
+        lax.fori_loop((b + 1) // 2, stop, column, 0)
+
+    def panel_step(b, first, last, stop):
+        here = pl.ds(pl.multiple_of(b * T, T), T)
+        block = z[here, here]
+
+        def between(i):
+            low_turn(3 * b + i)
+
+        done = invert_factor([block[G * g:G * (g + 1), :] for g in range(T // G)], between)
+        for g in range(T // G):
+            t_ref[b, G * g:G * (g + 1), :] = done[g]
+        inverse = t_ref[b]
+        scale_rows(here, inverse, jnp.maximum(first, (b + 1) // 3), last)
+        scale_rows(here, inverse, n_chunks, end_chunks)
+        update_rows(b, stop, [(first, last, True), (n_chunks, end_chunks, False)])
+
+    half_blocks = blocks // 2
+
+    def supernode(g, carry):
+        @pl.when(g == 1)
+        def _():
+            @pl.when(jnp.logical_not(low_source))
+            def _():
+                def rest(k, carry):
+                    pass_on(low, 1, k, c)
+                    return carry
+
+                lax.fori_loop(jnp.maximum(3 * half_blocks - lag, 0), pieces, rest, 0)
+
+            def settled(k, carry):
+                settle(low, 1, k, c, other)
+                return carry
+
+            lax.fori_loop(0, pieces, settled, 0)
+
+            def catch_up(b, carry):
+                here = pl.ds(pl.multiple_of(b * T, T), T)
+                scale_rows(here, t_ref[b], lead_chunks, n_chunks)
+                update_rows(b, half_blocks // 2, [(lead_chunks, n_chunks, False)])
+                return carry
+
+            lax.fori_loop(0, half_blocks, catch_up, 0)
+
+            def second(j, carry):
+                there = pl.ds(pl.multiple_of(width + j * 2 * T, 2 * T), 2 * T)
+                right = z[there, :width]
+
+                def update(i, carry):
+                    at = pl.ds(pl.multiple_of(i * chunk, chunk), chunk)
+                    z[at, there] = z[at, there] - dot_nt(z[at, :width], right)
+                    return carry
+
+                lax.fori_loop((width + j * 2 * T) // chunk, end_chunks, update, 0)
+                return carry
+
+            lax.fori_loop(0, half_blocks // 2, second, 0)
+
+        def step(i, carry):
+            panel_step(
+                g * half_blocks + i, g * lead_chunks, (g + 1) * lead_chunks,
+                (g + 1) * (half_blocks // 2))
+            return carry
+
+        lax.fori_loop(0, half_blocks, step, 0)
         return carry
 
-    lax.fori_loop(0, blocks, step, 0)
+    lax.fori_loop(0, 2, supernode, 0)
 
     for i in range(group):
         at = slice(n + i * B, n + (i + 1) * B)
@@ -290,10 +376,10 @@
         out_specs=pl.BlockSpec(memory_space=pltpu.VMEM),
         scratch_shapes=[
             pltpu.VMEM((n + share, n), jnp.float32),
-            pltpu.VMEM((T, T), jnp.float32),
+            pltpu.VMEM((n // T, T, T), jnp.float32),
             dma((2,)), dma((2,)),
-            dma((2, per_half)), dma((2, 2 * per_half)),
-            dma((4, per_half)), dma((4, 2 * per_half)),
+            dma((2, per_half)), dma((2, 4 * per_half)),
+            dma((4, per_half)), dma((4, 4 * per_half)),
             dma((2,)), dma((2,)),
         ],
         compiler_params=pltpu.CompilerParams(

time: 231 us -> 183 us (0.79)
  Pallas kernels: 225 us -> 176 us
    pallas_call x1, Pallas kernels: 225 us -> 176 us  [per_device(): pl.pallas_call(functools.partial(panel_kernel, counts), out_shape=jax.Sha...]
where the time goes in v4:
time: 183 us; the launch traced here: 182 us
  Pallas kernels  176 us (96%)
  local copies, waits for them, and re-layouts  5.99 us (3%)
    pallas_call x1, Pallas kernels, per_device(): pl.pallas_call(functools.partial(panel_kernel, counts), out_shape=jax.Sha...  176 us

profile of v4, /device:TPU:29, one launch (start us, length us, event | category | flops | bytes accessed | tf_op | source)
XLA Modules:
  0.0 182.4 jit_solution(15538822925303045449)
XLA Ops:
  0.0 0.8 copy.6
  0.8 0.1 fusion
  0.9 0.1 select_convert_fusion
  1.0 0.1 broadcast_in_dim.40
  1.0 0.1 reshape.19.mask_ref
  1.1 1.8 copy.9
  3.0 176.3 %shard_map.28 = f32[2,768,384]{2,1,0:T(8,128)S(1)} custom-call(f32[2,768,384]{2,1,0:T(8,128)S(1)} %bitcast.5, f32[8,1536]{1,0:T(8,128)S(1)} %reshape.19.mask_ref), custom_call_target="tpu_custom_call" | custom-call | tf_op jit(solution)/shard_map/pallas_call | solution.py:372
  179.2 3.2 %copy.7 = f32[768,2,384]{2,1,0:T(2,128)} copy(f32[768,2,384]{2,0,1:T(8,128)S(1)} %bitcast.4) | data formatting | bytes 4718592 | tf_op jit(solution)/shard_map/transpose | solution.py:389
  (2 shorter events, 0.0 us)

commit v5 on v4

--- a/solution.py
+++ b/solution.py
@@ -41,28 +41,46 @@
         here = jnp.logical_and(col >= G * p, col < G * (p + 1))
         unit = jnp.where(col == row + G * p, 1.0, 0.0).astype(jnp.float32)
         start = jnp.where(here, unit, a[p])
-        w = [subs(start, i) for i in range(G)]
-        inv, m = [], {}
-        for k in range(G):
-            r = 1.0 / s[k, k]
-            inv.append(r)
-            for i in range(k + 1, G):
-                m[i, k] = s[k, i] * r
-            for i in range(k + 1, G):
+        e = [lax.rsqrt(s[i, i]) for i in range(G)]
+        for i in range(G):
+            s[i, i] = 1.0
+            for j in range(i + 1, G):
+                s[i, j] = s[i, j] * (e[i] * e[j])
+        w = [subs(start, i) * e[i] for i in range(G)]
+        inv, m = {}, {}
+        done = None
+        for k in range(0, G, 2):
+            first, cross, last = s[k, k], s[k, k + 1], s[k + 1, k + 1]
+            det = first * last - cross * cross
+            r = 1.0 / det
+            inv[k] = (first, cross, last, r)
+            for i in range(k + 2, G):
+                m[i, k] = (s[k, i] * last - s[k + 1, i] * cross) * r
+                m[i, k + 1] = (s[k + 1, i] * first - s[k, i] * cross) * r
+            for i in range(k + 2, G):
                 for j in range(i, G):
-                    s[i, j] = s[i, j] - m[i, k] * s[k, j]
-            for i in range(k + 1, G):
-                w[i] = w[i] - m[i, k] * w[k]
-        done = w[0] * lax.rsqrt(s[0, 0])
-        for k in range(1, G):
-            done = jnp.where(row == k, w[k] * lax.rsqrt(s[k, k]), done)
+                    s[i, j] = s[i, j] - (m[i, k] * s[k, j] + m[i, k + 1] * s[k + 1, j])
+            for i in range(k + 2, G):
+                w[i] = w[i] - (m[i, k] * w[k] + m[i, k + 1] * w[k + 1])
+        for k in range(0, G, 2):
+            first, cross, last, r = inv[k]
+            det = first * last - cross * cross
+            upper = w[k] if k == 0 else w[k] * lax.rsqrt(first)
+            under = (first * w[k + 1] - cross * w[k]) * lax.rsqrt(first * det)
+            done = upper if k == 0 else jnp.where(row == k, upper, done)
+            done = jnp.where(row == k + 1, under, done)
         out.append(jnp.where(col < G * (p + 1), done, 0.0))
         if p == count - 1:
             break
-        w = [w[k] * inv[k] for k in range(G)]
-        for k in range(G - 1, 0, -1):
+        v = [None] * G
+        for k in range(0, G, 2):
+            first, cross, last, r = inv[k]
+            v[k] = (last * w[k] - cross * w[k + 1]) * r
+            v[k + 1] = (first * w[k + 1] - cross * w[k]) * r
+        for k in range(G - 2, 0, -2):
             for i in range(k):
-                w[i] = w[i] - m[k, i] * w[k]
+                v[i] = v[i] - (m[k, i] * v[k] + m[k + 1, i] * v[k + 1])
+        w = [v[k] * e[k] for k in range(G)]
         for g in range(p + 1, count):
             part = [lanes(a[g], G * p + k) * w[k] for k in range(G)]
             while len(part) > 1:
@@ -108,9 +126,12 @@
     pl.semaphore_wait(barrier, heard)
 
     def lead(k, cc, dest, slot, root):
-        column = cc * per_half + k
-        there = z.at[pl.ds(column * T, width - column * T), pl.ds(column * T, T)]
-        near = p_ref.at[0, pl.ds(column * T, width - column * T), pl.ds(k * T, T)]
+        own, piece = k // 4, k % 4
+        column = cc * per_half + own
+        length = (width - column * T) // 4
+        down = pl.ds(column * T + piece * length, length)
+        there = z.at[down, pl.ds(column * T, T)]
+        near = p_ref.at[0, down, pl.ds(own * T, T)]
         return pltpu.make_async_remote_copy(
             src_ref=near if root else there, dst_ref=there, send_sem=a_send.at[slot, k],
             recv_sem=a_recv.at[cc, k], **dest)
@@ -192,12 +213,12 @@
         def _():
             @pl.when(jnp.logical_and(side == 0, q == 0))
             def _():
-                for k in range(per_half):
+                for k in range(4 * per_half):
                     fan_out(lead, k, cc, True)
 
             @pl.when(jnp.logical_or(side != 0, q != 0))
             def _():
-                for k in range(per_half):
+                for k in range(4 * per_half):
                     pass_on(lead, 0, k, cc)
 
     @pl.when(low_source)
@@ -220,7 +241,7 @@
             def _():
                 z[:width, cc * half:(cc + 1) * half] = p_ref[0]
 
-            for k in range(per_half):
+            for k in range(4 * per_half):
                 settle(lead, 0, k, cc, 1 - cc)
 
     @pl.when(low_source)
@@ -378,8 +399,8 @@
             pltpu.VMEM((n + share, n), jnp.float32),
             pltpu.VMEM((n // T, T, T), jnp.float32),
             dma((2,)), dma((2,)),
-            dma((2, per_half)), dma((2, 4 * per_half)),
-            dma((4, per_half)), dma((4, 4 * per_half)),
+            dma((2, 4 * per_half)), dma((2, 4 * per_half)),
+            dma((4, 4 * per_half)), dma((4, 4 * per_half)),
             dma((2,)), dma((2,)),
         ],
         compiler_params=pltpu.CompilerParams(

time: 183 us -> 172 us (0.940)
  Pallas kernels: 176 us -> 165 us
    pallas_call x1, Pallas kernels: 176 us -> 165 us  [per_device(): pl.pallas_call(functools.partial(panel_kernel, counts), out_shape=jax.Sha...]
where the time goes in v5:
time: 172 us; the launch traced here: 171 us
  Pallas kernels  165 us (96%)
  local copies, waits for them, and re-layouts  5.99 us (3%)
    pallas_call x1, Pallas kernels, per_device(): pl.pallas_call(functools.partial(panel_kernel, counts), out_shape=jax.Sha...  165 us

profile of v5, /device:TPU:29, one launch (start us, length us, event | category | flops | bytes accessed | tf_op | source)
XLA Modules:
  0.0 171.4 jit_solution(16054113322901360187)
XLA Ops:
  0.0 0.8 copy.6
  0.8 0.1 fusion
  0.9 0.1 select_convert_fusion
  1.0 0.1 broadcast_in_dim.40
  1.0 0.1 reshape.19.mask_ref
  1.1 1.8 %copy.9 = f32[768,2,384]{2,0,1:T(8,128)S(1)} copy(f32[768,2,384]{2,1,0:T(2,128)} %param.2) | data formatting | bytes 4718592 | tf_op args[0]
  3.0 165.2 %shard_map.28 = f32[2,768,384]{2,1,0:T(8,128)S(1)} custom-call(f32[2,768,384]{2,1,0:T(8,128)S(1)} %bitcast.5, f32[8,1536]{1,0:T(8,128)S(1)} %reshape.19.mask_ref), custom_call_target="tpu_custom_call" | custom-call | tf_op jit(solution)/shard_map/pallas_call | solution.py:393
  168.1 3.2 %copy.7 = f32[768,2,384]{2,1,0:T(2,128)} copy(f32[768,2,384]{2,0,1:T(8,128)S(1)} %bitcast.4) | data formatting | bytes 4718592 | tf_op jit(solution)/shard_map/transpose | solution.py:410
  (2 shorter events, 0.0 us)
